TPU v7x, 32 devices: a whole 2x2x4 slice. The times are simulated.
32 devices in a mesh: au: 4 (over y, x), ia: 8 (over z, core).
Axes of the slice: x: 2, y: 2, z: 4, core: 2. Of those that a mesh axis runs over, the one named last changes fastest.
Arguments:
- user_emb: bfloat16 [4096, 128], P(('au', 'ia')), may hold values from -1.75 to 1.75
- item_emb: bfloat16 [16384, 128], P(('au', 'ia')), may hold values from -1.75 to 1.75
- user_cot: bfloat16 [4096, 128], P(('au', 'ia')), may hold values from -6 to 6
- item_cot: bfloat16 [16384, 128], P(('au', 'ia')), may hold values from -6 to 6
- user_degree: int32 [4096], P('au'), may hold values from 8 to 31
- item_degree: int32 [4, 8, 512], P(None, 'ia'), may hold values from 2 to 7
- tile_rows: int32 [4, 8, 24], P('au', 'ia'), may hold values from 0 to 3, as said below
- tile_cols: int32 [4, 8, 24], P('au', 'ia'), may hold values from 0 to 7
- tile_key: int32 [4, 8, 24], P('au', 'ia'), may hold values from 0 to 4095
- tile_count: int32 [4, 8], P('au', 'ia'), may hold values from 1 to 24, as said below
Outputs:
- user_final: bfloat16 [4096, 128], P(('au', 'ia'))
- item_final: bfloat16 [16384, 128], P(('au', 'ia'))
- user_grad: float32 [4096, 128], P(('au', 'ia'))
- item_grad: float32 [16384, 128], P(('au', 'ia'))
Inputs may be any that keep to these rules, and one draw needn't show every extreme that they name: On each device the first tile_count entries of tile_rows and tile_cols name distinct tiles; later entries are not read. `tile_count`: some device has exactly 24 occupied tiles in every draw.
All inputs are finite; a program needn't handle non-finite values.
Results may differ from a plain program's by a relative error of at most 0.012.
Values may be sent and summed in bfloat16 or wider, within the bound.
A program may use at most 64 MiB of HBM per device.

v0:
```python
import jax
import jax.numpy as jnp
from jax import lax
from jax.sharding import PartitionSpec as P

EMB = 128
TILE = 256


def edge_mask(size, tile_number):
    row_ids = lax.broadcasted_iota(jnp.int32, (size, size), 0)
    col_ids = lax.broadcasted_iota(jnp.int32, (size, size), 1)
    hashed = (row_ids * 977 + tile_number * 263) % 8191
    hashed = (hashed * hashed % 8191 + col_ids * 1531) % 8191
    hashed = hashed * hashed % 8191
    return jnp.where(hashed % 8 == 0, 1.0, 0.0).astype(jnp.float32)


def gate_weight(user_rows, item_rows, user_norm, item_norm, tile_number):
    logits = lax.dot_general(
        user_rows, item_rows, (((1,), (1,)), ((), ())), preferred_element_type=jnp.float32
    )
    gate_value = jax.nn.sigmoid(logits)
    weight = edge_mask(user_rows.shape[0], tile_number) / jnp.sqrt(
        user_norm[:, None] * item_norm[None, :]
    )
    return (gate_value, weight)


def left_product(matrix, other):
    return lax.dot_general(
        matrix, other, (((0,), (0,)), ((), ())), preferred_element_type=jnp.float32
    )


def right_product(matrix, other):
    return lax.dot_general(
        matrix, other, (((1,), (1,)), ((), ())), preferred_element_type=jnp.float32
    )


def add_block(running, offset, addend):
    current = lax.dynamic_slice_in_dim(running, offset, addend.shape[0], 0)
    return lax.dynamic_update_slice_in_dim(running, current + addend, offset, 0)


def per_device(
    user_emb,
    item_emb,
    user_cot,
    item_cot,
    user_degree,
    item_degree,
    tile_rows,
    tile_cols,
    tile_key,
    tile_count,
):
    user_norm = user_degree.astype(jnp.float32)
    item_norm = item_degree.reshape(-1).astype(jnp.float32)
    row_ids = tile_rows.reshape(-1)
    col_ids = tile_cols.reshape(-1)
    key_ids = tile_key.reshape(-1)
    occupied = tile_count.reshape(-1)[0]

    def gather_users(shard):
        return lax.all_gather(shard, "ia", axis=0, tiled=True)

    def gather_items(shard):
        return lax.all_gather(shard, "au", axis=0, tiled=True)

    def sum_users(partial_sum):
        return lax.psum_scatter(
            partial_sum.astype(jnp.bfloat16), "ia", scatter_dimension=0, tiled=True
        ).astype(jnp.float32)

    def sum_items(partial_sum):
        return lax.psum_scatter(
            partial_sum.astype(jnp.bfloat16), "au", scatter_dimension=0, tiled=True
        ).astype(jnp.float32)

    first_users = gather_users(jnp.concatenate([user_emb, user_cot], axis=1))
    first_items = gather_items(jnp.concatenate([item_emb, item_cot], axis=1))
    user_zeros = jnp.zeros((first_users.shape[0], 2 * EMB), jnp.float32)
    item_zeros = jnp.zeros((first_items.shape[0], 2 * EMB), jnp.float32)

    def tile_starts(slot_index):
        return (row_ids[slot_index] * TILE, col_ids[slot_index] * TILE)

    def first_tile(slot_index):
        user_start, item_start = tile_starts(slot_index)
        first_user = lax.dynamic_slice_in_dim(first_users, user_start, TILE, 0)
        first_item = lax.dynamic_slice_in_dim(first_items, item_start, TILE, 0)
        gate_value, weight = gate_weight(
            first_user[:, :EMB],
            first_item[:, :EMB],
            lax.dynamic_slice_in_dim(user_norm, user_start, TILE, 0),
            lax.dynamic_slice_in_dim(item_norm, item_start, TILE, 0),
            key_ids[slot_index],
        )
        adjacency = (gate_value * weight).astype(jnp.bfloat16)
        return (user_start, item_start, first_user, first_item, gate_value, weight, adjacency)

    def first_joint(slot_index, partials):
        user_start, item_start, first_user, first_item, gate_value, weight, adjacency = first_tile(
            slot_index
        )
        user_term = jnp.dot(adjacency, first_item, preferred_element_type=jnp.float32)
        item_term = left_product(adjacency, first_user)
        return (
            add_block(partials[0], user_start, user_term),
            add_block(partials[1], item_start, item_term),
        )

    user_first, item_first = lax.fori_loop(0, occupied, first_joint, (user_zeros, item_zeros))
    shard_sum = sum_users(user_first)
    layer_shard = shard_sum[:, :EMB].astype(jnp.bfloat16)
    back_shard = (user_cot.astype(jnp.float32) + shard_sum[:, EMB:]).astype(jnp.bfloat16)
    later_users = gather_users(jnp.concatenate([layer_shard, back_shard], axis=1))
    shard_sum = sum_items(item_first)
    finish_layer_shard = shard_sum[:, :EMB].astype(jnp.bfloat16)
    back_shard = (item_cot.astype(jnp.float32) + shard_sum[:, EMB:]).astype(jnp.bfloat16)
    later_items = gather_items(jnp.concatenate([finish_layer_shard, back_shard], axis=1))

    def second_tile(slot_index):
        user_start, item_start, first_user, first_item, gate_value, weight, adjacency = first_tile(
            slot_index
        )
        later_user = lax.dynamic_slice_in_dim(later_users, user_start, TILE, 0)
        later_item = lax.dynamic_slice_in_dim(later_items, item_start, TILE, 0)
        slope = right_product(first_user[:, :EMB], later_item[:, EMB:])
        slope = slope + right_product(first_user[:, EMB:], later_item[:, :EMB])
        slope = slope + right_product(later_user[:, :EMB], first_item[:, EMB:])
        slope = slope + right_product(later_user[:, EMB:], first_item[:, :EMB])
        descent = (slope * weight * gate_value * (1.0 - gate_value)).astype(jnp.bfloat16)
        return (
            user_start,
            item_start,
            first_user,
            first_item,
            later_user,
            later_item,
            adjacency,
            descent,
        )

    def user_term_of(adjacency, descent, first_item, later_item):
        product = jnp.dot(adjacency, later_item, preferred_element_type=jnp.float32)
        extra = jnp.dot(descent, first_item[:, :EMB], preferred_element_type=jnp.float32)
        return jnp.concatenate([product[:, :EMB], product[:, EMB:] + extra], axis=1)

    def item_term_of(adjacency, descent, first_user, later_user):
        product = left_product(adjacency, later_user)
        extra = left_product(descent, first_user[:, :EMB])
        return jnp.concatenate([product[:, :EMB], product[:, EMB:] + extra], axis=1)

    def second_joint(slot_index, partials):
        (
            user_start,
            item_start,
            first_user,
            first_item,
            later_user,
            later_item,
            adjacency,
            descent,
        ) = second_tile(slot_index)
        return (
            add_block(
                partials[0], user_start, user_term_of(adjacency, descent, first_item, later_item)
            ),
            add_block(
                partials[1], item_start, item_term_of(adjacency, descent, first_user, later_user)
            ),
        )

    user_second, item_second = lax.fori_loop(0, occupied, second_joint, (user_zeros, item_zeros))
    user_done = sum_users(user_second)
    item_done = sum_items(item_second)
    user_final = (
        (user_emb.astype(jnp.float32) + layer_shard.astype(jnp.float32) + user_done[:, :EMB]) / 3.0
    ).astype(jnp.bfloat16)
    user_grad = (user_cot.astype(jnp.float32) + user_done[:, EMB:]) / 3.0
    item_final = (
        (item_emb.astype(jnp.float32) + finish_layer_shard.astype(jnp.float32) + item_done[:, :EMB])
        / 3.0
    ).astype(jnp.bfloat16)
    item_grad = (item_cot.astype(jnp.float32) + item_done[:, EMB:]) / 3.0
    return (user_final, item_final, user_grad, item_grad)


def solution(mesh):
    in_specs = (
        P(("au", "ia"), None),
        P(("au", "ia"), None),
        P(("au", "ia"), None),
        P(("au", "ia"), None),
        P("au"),
        P(None, "ia", None),
        P("au", "ia", None),
        P("au", "ia", None),
        P("au", "ia", None),
        P("au", "ia"),
    )
    out_specs = (
        P(("au", "ia"), None),
        P(("au", "ia"), None),
        P(("au", "ia"), None),
        P(("au", "ia"), None),
    )
    return jax.shard_map(
        per_device, mesh=mesh, in_specs=in_specs, out_specs=out_specs, check_vma=False
    )
```

profile of v0, /device:TPU:9, one launch (start us, length us, event | category | flops | bytes accessed | tf_op | source)
XLA Modules:
  0.0 852.7 jit_solution(5952517412885560503)
XLA Ops:
  11.2 16.5 %all_gather.12 = bf16[1024,256]{1,0:T(8,128)(2,1)} all-gather(bf16[128,256]{1,0:T(8,128)(2,1)S(1)} %pad_maximum_fusion.2), channel_id=1, replica_groups=mesh['au'=4,'ia'=8] {'ia'}, dimensions={0}, use_global_device_ids=true | all-gather | bytes 589824 | tf_op jit(solution)/shard_map/all_gather | solution.py:67
  27.6 10.6 %all-gather.3.cloned.1.call-done = bf16[2048,256]{1,0:T(8,128)(2,1)} async-done(((bf16[512,256]{1,0:T(8,128)(2,1)}), bf16[2048,256]{1,0:T(8,128)(2,1)}) %all-gather.3.cloned.1.call-update) | async-done | bytes 1048592 | tf_op jit(solution)/shard_map/all_gather | solution.py:70
  38.5 186.0 %while.30 = (s32[]{:T(128)}, f32[1024,256]{1,0:T(8,128)S(1)}, f32[2048,256]{1,0:T(8,128)S(1)}, s32[]{:T(128)}, s32[24]{0:T(128)S(1)}, /*index=5*/bf16[1024,256]{...) while((s32[]{:T(128)}, f32[1024,256]{1,0:T(8,128)S(1)}, ...), condition=%wide.region_1.2_spmd, body=%wide.region_0.1_spmd.sunk | while | flops 86772496 | bytes 1848195 | solution.py:115
  226.6 43.8 %reduce-scatter.7.cloned.1.call-done = bf16[512,256]{1,0:T(8,128)(2,1)} async-done(((bf16[2048,256]{1,0:T(8,128)(2,1)}), bf16[512,256]{1,0:T(8,128)(2,1)}) %reduce-scatter.7.cloned.1.call-update) | async-done | bytes 262160 | tf_op jit(solution)/shard_map/reduce_scatter | solution.py:78
  273.0 23.9 %reduce-scatter.5.cloned.1.call-done = bf16[128,256]{1,0:T(8,128)(2,1)} async-done(((bf16[1024,256]{1,0:T(8,128)(2,1)}), bf16[128,256]{1,0:T(8,128)(2,1)}) %reduce-scatter.5.cloned.1.call-update) | async-done | bytes 65552 | tf_op jit(solution)/shard_map/reduce_scatter | solution.py:73
  298.5 20.4 %all_gather.15 = bf16[1024,256]{1,0:T(8,128)(2,1)} all-gather(bf16[128,256]{1,0:T(8,128)(2,1)S(1)} %pad_maximum_fusion.3), channel_id=1, replica_groups=mesh['au'=4,'ia'=8] {'ia'}, dimensions={0}, use_global_device_ids=true | all-gather | bytes 589824 | tf_op jit(solution)/shard_map/all_gather | solution.py:67
  318.8 11.9 %all-gather.5.cloned.1.call-done = bf16[2048,256]{1,0:T(8,128)(2,1)} async-done(((bf16[512,256]{1,0:T(8,128)(2,1)}), bf16[2048,256]{1,0:T(8,128)(2,1)}) %all-gather.5.cloned.1.call-update) | async-done | bytes 1048592 | tf_op jit(solution)/shard_map/all_gather | solution.py:70
  331.9 412.6 %while.31 = (s32[]{:T(128)}, f32[1024,256]{1,0:T(8,128)}, f32[2048,256]{1,0:T(8,128)S(1)}, s32[]{:T(128)}, s32[24]{0:T(128)S(1)}, /*index=5*/bf16[1024,256]{1,0:...) while((s32[]{:T(128)}, f32[1024,256]{1,0:T(8,128)}, ...), condition=%wide.region_5.6_spmd, body=%wide.region_4.5_spmd.sunk | while | flops 193138192 | bytes 12607007 | solution.py:177
  339.4 1.8 fusion.135
  358.1 1.8 fusion.135
  376.8 1.8 fusion.135
  395.5 1.8 fusion.135
  414.3 1.8 fusion.135
  433.0 1.8 fusion.135
  451.7 1.8 fusion.135
  470.4 1.8 fusion.135
  489.2 1.8 fusion.135
  507.9 1.8 fusion.135
  526.6 1.8 fusion.135
  545.3 1.8 fusion.135
  564.1 1.8 fusion.135
  582.8 1.8 fusion.135
  601.5 1.8 fusion.135
  620.2 1.8 fusion.135
  638.9 1.8 fusion.135
  657.7 1.8 fusion.135
  676.4 1.8 fusion.135
  695.1 1.8 fusion.135
  713.8 1.8 fusion.135
  744.5 2.1 convert_element_type.95
  747.8 60.6 %reduce-scatter.9.cloned.1.call-done = bf16[128,256]{1,0:T(8,128)(2,1)} async-done(((bf16[1024,256]{1,0:T(8,128)(2,1)}), bf16[128,256]{1,0:T(8,128)(2,1)}) %reduce-scatter.9.cloned.1.call-update) | async-done | bytes 65552 | tf_op jit(solution)/shard_map/reduce_scatter | solution.py:73
  809.9 34.1 %reduce-scatter.11.cloned.1.call-done = bf16[512,256]{1,0:T(8,128)(2,1)} async-done(((bf16[2048,256]{1,0:T(8,128)(2,1)}), bf16[512,256]{1,0:T(8,128)(2,1)}) %reduce-scatter.11.cloned.1.call-update) | async-done | bytes 262160 | tf_op jit(solution)/shard_map/reduce_scatter | solution.py:78
  (976 shorter events, 455.1 us)
Async XLA Ops:
  7.2 31.1 %all-gather.3.cloned.1.call-start = ((), (), s32[]{:S(2)}) async-start(), calls=%async_computation.4 | async-start | bytes 1310720 | tf_op jit(solution)/shard_map/all_gather | solution.py:70
  8.9 29.5 %copy-start.7 = (s32[1,1,24]{2,1,0:T(1,128)S(1)}, s32[1,1,24]{2,1,0:T(1,128)}, u32[]{:S(2)}) copy-start(s32[1,1,24]{2,1,0:T(1,128)} %param.20) | copy-start | bytes 292
  8.9 29.6 %copy-start.8 = (s32[1,1,24]{2,1,0:T(1,128)S(1)}, s32[1,1,24]{2,1,0:T(1,128)}, u32[]{:S(2)}) copy-start(s32[1,1,24]{2,1,0:T(1,128)} %param.21) | copy-start | bytes 292
  8.9 29.6 %copy-start.9 = (s32[1,1,24]{2,1,0:T(1,128)S(1)}, s32[1,1,24]{2,1,0:T(1,128)}, u32[]{:S(2)}) copy-start(s32[1,1,24]{2,1,0:T(1,128)} %param.22) | copy-start | bytes 292
  8.9 261.4 %reduce-scatter.7.cloned.1.call-start = ((), (), s32[]{:S(2)}) async-start(), calls=%async_computation.6 | async-start | bytes 1310720 | tf_op jit(solution)/shard_map/reduce_scatter | solution.py:78
  225.6 45.7 %copy-start.1 = (bf16[512,128]{1,0:T(8,128)(2,1)S(1)}, bf16[512,128]{1,0:T(8,128)(2,1)}, u32[]{:S(2)}) copy-start(bf16[512,128]{1,0:T(8,128)(2,1)} %param.17) | copy-start | bytes 393220
  225.6 72.1 %copy-start.4 = (bf16[128,128]{1,0:T(8,128)(2,1)S(1)}, bf16[128,128]{1,0:T(8,128)(2,1)}, u32[]{:S(2)}) copy-start(bf16[128,128]{1,0:T(8,128)(2,1)} %param.16) | copy-start | bytes 98308
  225.6 71.3 %reduce-scatter.5.cloned.1.call-start = ((), (), s32[]{:S(2)}) async-start(), calls=%async_computation.5 | async-start | bytes 589824 | tf_op jit(solution)/shard_map/reduce_scatter | solution.py:73
  226.5 104.2 %all-gather.5.cloned.1.call-start = ((), (), s32[]{:S(2)}) async-start(), calls=%async_computation.7 | async-start | bytes 1310720 | tf_op jit(solution)/shard_map/all_gather | solution.py:70
  273.0 535.4 %reduce-scatter.9.cloned.1.call-start = ((), (), s32[]{:S(2)}) async-start(), calls=%async_computation.8 | async-start | bytes 589824 | tf_op jit(solution)/shard_map/reduce_scatter | solution.py:73
  339.4 6.7 copy-start
  358.1 6.7 copy-start
  395.5 6.7 copy-start
  414.2 6.7 copy-start
  451.7 6.7 copy-start
  470.4 6.7 copy-start
  507.9 6.7 copy-start
  526.6 6.7 copy-start
  545.3 6.7 copy-start
  564.0 6.7 copy-start
  582.8 6.7 copy-start
  601.5 6.7 copy-start
  638.9 6.7 copy-start
  657.6 6.7 copy-start
  676.4 6.7 copy-start
  695.1 6.7 copy-start
  713.8 6.7 copy-start
  746.6 97.5 %reduce-scatter.11.cloned.1.call-start = ((), (), s32[]{:S(2)}) async-start(), calls=%async_computation.9 | async-start | bytes 1310720 | tf_op jit(solution)/shard_map/reduce_scatter | solution.py:78
  746.6 62.6 %copy-start.5 = (bf16[128,256]{1,0:T(8,128)(2,1)S(1)}, bf16[128,256]{1,0:T(8,128)(2,1)}, u32[]{:S(2)}) copy-start(bf16[128,256]{1,0:T(8,128)(2,1)} %reduce-scatter.5.cloned.1.call-done) | copy-start | bytes 196612
  746.6 62.6 %copy-start.6 = (bf16[128,128]{1,0:T(8,128)(2,1)S(1)}, bf16[128,128]{1,0:T(8,128)(2,1)}, u32[]{:S(2)}) copy-start(bf16[128,128]{1,0:T(8,128)(2,1)} %param.14) | copy-start | bytes 98308
  746.6 98.4 %copy-start.2 = (bf16[512,256]{1,0:T(8,128)(2,1)S(1)}, bf16[512,256]{1,0:T(8,128)(2,1)}, u32[]{:S(2)}) copy-start(bf16[512,256]{1,0:T(8,128)(2,1)} %reduce-scatter.7.cloned.1.call-done) | copy-start | bytes 786436
  746.6 98.4 %copy-start.3 = (bf16[512,128]{1,0:T(8,128)(2,1)S(1)}, bf16[512,128]{1,0:T(8,128)(2,1)}, u32[]{:S(2)}) copy-start(bf16[512,128]{1,0:T(8,128)(2,1)} %param.15) | copy-start | bytes 393220
  (27 other events, 90.1 us)
Sparse Core Ops, SparseCore 0:
  10.4 27.7 all-gather.2
  225.7 44.5 reduce-scatter.6
  272.7 24.1 reduce-scatter.4
  299.2 31.4 all-gather.4
  746.7 61.6 reduce-scatter.8
  811.4 32.6 reduce-scatter.10
where the time goes:
time: 868 us; the launch traced here: 853 us
  matrix products  339 us (39%)
  waiting for transfers between devices  185 us (21%)
  local copies, waits for them, and re-layouts  138 us (16%)
  loops' own time  122 us (14%)
  blocking collectives  36.8 us (4%)
  other arithmetic  18.2 us (2%)
  between operations  14.3 us (2%)
    dot_general x88, matrix products, right_product(): lax.dot_general(matrix, other, (((1,), (1,)), ((), ())), preferred_elemen...  105 us
    dot_general x66, matrix products, left_product(): lax.dot_general(matrix, other, (((0,), (0,)), ((), ())), preferred_elemen...  89.1 us
    reduce_scatter x2, waiting for transfers between devices, sum_users(): lax.psum_scatter(partial_sum.astype(jnp.bfloat16), 'ia', scatter_dimensio...  84.5 us
    reduce_scatter x2, waiting for transfers between devices, sum_items(): lax.psum_scatter(partial_sum.astype(jnp.bfloat16), 'au', scatter_dimensio...  77.9 us
    another operation x1, loops' own time, per_device(): lax.fori_loop(0, occupied, second_joint, (user_zeros, item_zeros))  62.5 us
    another operation x1, loops' own time, per_device(): lax.fori_loop(0, occupied, first_joint, (user_zeros, item_zeros))  59.1 us
    dot_general x44, matrix products, gate_weight(): lax.dot_general(user_rows, item_rows, (((1,), (1,)), ((), ())), preferred...  59.1 us
    dynamic_slice x88, local copies, waits for them, and re-layouts, tile_starts(): return (row_ids[slot_index] * TILE, col_ids[slot_index] * TILE)  51.7 us
  transfers between devices with their start and end apart: 6, of which 6 were waited for; matrix products, arithmetic and copies ran while one was open for 1% of the time, Pallas kernels for 0%

commit v1 on v0

v1 whole, which is shorter than its diff:
```python
import functools

import jax
import jax.numpy as jnp
from jax import lax
from jax.experimental import pallas as pl
from jax.experimental.pallas import tpu as pltpu
from jax.sharding import PartitionSpec as P

EMB = 128
TILE = 256
MESH = pl.DeviceIdType.MESH
F32 = jnp.float32
BF16 = jnp.bfloat16


def nt_dot(left, right):
    return lax.dot_general(left, right, (((1,), (1,)), ((), ())), preferred_element_type=F32)


def nn_dot(left, right):
    return jnp.dot(left, right, preferred_element_type=F32)


def kernel(
    n_au,
    n_ia,
    keys,
    user_emb,
    item_emb,
    user_cot,
    item_cot,
    user_degree,
    item_degree,
    user_final,
    item_final,
    user_grad,
    item_grad,
    users,
    items,
    later_users,
    later_items,
    users_t,
    later_users_t,
    weight,
    adjacency,
    user_scale,
    item_scale,
    user_sum,
    item_sum,
    user_stage,
    item_stage,
    user_recv,
    item_recv,
    user_send_sem,
    user_recv_sem,
    item_send_sem,
    item_recv_sem,
):
    a = lax.axis_index("au")
    i = lax.axis_index("ia")
    us = user_emb.shape[0]
    it = item_emb.shape[0]
    u_block = us * n_ia
    i_block = it * n_au
    u_tiles = u_block // TILE
    i_tiles = i_block // TILE
    chunk = max(TILE, it)
    chunks = i_block // chunk
    chunk_tiles = chunk // TILE
    chunk_peers = chunk // it

    def rows(index, size):
        return pl.ds(pl.multiple_of(index * size, size), size)

    my_users = rows(i, us)
    my_items = rows(a, it)

    users[my_users, :EMB] = user_emb[...]
    users[my_users, EMB:] = user_cot[...]
    items[my_items, :EMB] = item_cot[...]
    items[my_items, EMB:] = item_emb[...]

    barrier = pltpu.get_barrier_semaphore()
    for d in range(1, n_ia):
        pl.semaphore_signal(barrier, inc=1, device_id=(a, lax.rem(i + d, n_ia)), device_id_type=MESH)
    for d in range(1, n_au):
        pl.semaphore_signal(barrier, inc=1, device_id=(lax.rem(a + d, n_au), i), device_id_type=MESH)
    pl.semaphore_wait(barrier, n_ia + n_au - 2)

    def spread_users(ref, phase, d):
        return pltpu.make_async_remote_copy(
            src_ref=ref.at[my_users],
            dst_ref=ref.at[my_users],
            send_sem=user_send_sem.at[phase, d],
            recv_sem=user_recv_sem.at[phase, d],
            device_id=(a, lax.rem(i + d, n_ia)),
            device_id_type=MESH,
        )

    def spread_items(ref, phase, d):
        return pltpu.make_async_remote_copy(
            src_ref=ref.at[my_items],
            dst_ref=ref.at[my_items],
            send_sem=item_send_sem.at[phase, d],
            recv_sem=item_recv_sem.at[phase, d],
            device_id=(lax.rem(a + d, n_au), i),
            device_id_type=MESH,
        )

    def user_part(layer, d):
        peer = lax.rem(i + d, n_ia)
        return pltpu.make_async_remote_copy(
            src_ref=user_stage.at[layer, rows(peer, us)],
            dst_ref=user_recv.at[layer, d],
            send_sem=user_send_sem.at[2 * layer + 1, d],
            recv_sem=user_recv_sem.at[2 * layer + 1, d],
            device_id=(a, peer),
            device_id_type=MESH,
        )

    def item_part(layer, d):
        peer = lax.rem(a + d, n_au)
        return pltpu.make_async_remote_copy(
            src_ref=item_stage.at[layer, rows(peer, it)],
            dst_ref=item_recv.at[layer, d],
            send_sem=item_send_sem.at[2 * layer + 1, d],
            recv_sem=item_recv_sem.at[2 * layer + 1, d],
            device_id=(peer, i),
            device_id_type=MESH,
        )

    for d in range(1, n_ia):
        spread_users(users, 0, d).start()
    for d in range(1, n_au):
        spread_items(items, 0, d).start()

    scale_row = lax.rsqrt(user_degree[...].astype(F32))
    for r in range(u_tiles):
        part = scale_row[:, r * TILE : (r + 1) * TILE]
        user_scale[r * TILE : (r + 1) * TILE, :] = jnp.transpose(
            jnp.broadcast_to(part, (128, TILE))
        )
    for p in range(n_au):
        item_scale[:, p * it : (p + 1) * it] = lax.rsqrt(item_degree[p].astype(F32))

    row_ids = lax.broadcasted_iota(jnp.int32, (TILE, 128), 0) * 977
    col_ids = lax.broadcasted_iota(jnp.int32, (1, TILE), 1) * 1531
    col_ids = lax.rem(col_ids, 8191) - 8191

    def fold(value):
        return (value & 8191) + (value >> 13)

    def mask_tile(t, carry):
        r = t // i_tiles
        c = t % i_tiles
        key = keys[t]
        target = jnp.where(key >= 0, 0, 8)
        h1 = fold(row_ids + key * 263)
        h1 = jnp.where(h1 >= 8191, h1 - 8191, h1)
        h1 = fold(h1 * h1)
        h1 = jnp.where(h1 >= 8191, h1 - 8191, h1)
        scale = user_scale[rows(r, TILE), :]
        for half in range(TILE // 128):
            lanes = slice(half * 128, (half + 1) * 128)
            h2 = h1 + col_ids[:, lanes]
            h3 = fold(h2 * h2)
            h3 = jnp.where(h3 >= 8191, h3 + 1, h3) & 7
            where = pl.ds(pl.multiple_of(c * TILE + half * 128, 128), 128)
            weight[rows(r, TILE), where] = jnp.where(
                h3 == target, scale * item_scale[:, where], 0.0
            )
        return carry

    lax.fori_loop(0, u_tiles * i_tiles, mask_tile, 0)

    user_sum[...] = jnp.zeros_like(user_sum)
    for d in range(1, n_ia):
        spread_users(users, 0, d).wait_recv()
    for r in range(u_tiles):
        users_t[:, r * TILE : (r + 1) * TILE] = jnp.transpose(users[r * TILE : (r + 1) * TILE, :])
    for d in range(1, n_au):
        spread_items(items, 0, d).wait_recv()

    def send_chunk(layer, k):
        for p in range(chunk_peers):
            peer = k * chunk_peers + p
            item_stage[layer, rows(peer, it), :] = jnp.transpose(
                item_sum[:, p * it : (p + 1) * it]
            ).astype(BF16)

            @pl.when(peer != a)
            def _():
                item_part(layer, lax.rem(peer - a + n_au, n_au)).start()

    def first_chunk(j, carry):
        k = lax.rem(a // chunk_peers + 1 + j, chunks)
        item_sum[...] = jnp.zeros_like(item_sum)

        def tile(t, inner):
            r = t // chunk_tiles
            c = t % chunk_tiles
            at_user = rows(r, TILE)
            at_item = rows(k * chunk_tiles + c, TILE)
            own_item = items[at_item, :]
            gate = jax.nn.sigmoid(nt_dot(users[at_user, :EMB], own_item[:, EMB:]))
            adj = gate * weight[at_user, at_item]
            weight[at_user, at_item] = adj * (1.0 - gate)
            adj = adj.astype(BF16)
            adjacency[at_user, at_item] = adj
            user_sum[at_user, :] += nn_dot(adj, own_item)
            item_sum[:, rows(c, TILE)] += nn_dot(users_t[:, at_user], adj)
            return inner

        lax.fori_loop(0, u_tiles * chunk_tiles, tile, 0)
        send_chunk(0, k)
        return carry

    lax.fori_loop(0, chunks, first_chunk, 0)

    user_stage[0] = user_sum[...].astype(BF16)
    for d in range(1, n_ia):
        user_part(0, d).start()

    def user_total(layer):
        total = user_stage[layer, my_users, :].astype(F32)
        for d in range(1, n_ia):
            user_part(layer, d).wait_recv()
            total = total + user_recv[layer, d].astype(F32)
        return total

    def item_total(layer):
        for d in range(1, n_au):
            item_part(layer, d).wait_recv()
        total = item_stage[layer, my_items, :].astype(F32)
        for d in range(1, n_au):
            total = total + item_recv[layer, d].astype(F32)
        return total

    total = item_total(0)
    later_items[my_items, :EMB] = (item_cot[...].astype(F32) + total[:, EMB:]).astype(BF16)
    later_items[my_items, EMB:] = total[:, :EMB].astype(BF16)
    for d in range(1, n_au):
        spread_items(later_items, 2, d).start()
    total = user_total(0)
    later_users[my_users, :EMB] = total[:, EMB:].astype(BF16)
    later_users[my_users, EMB:] = (user_cot[...].astype(F32) + total[:, :EMB]).astype(BF16)
    for d in range(1, n_ia):
        spread_users(later_users, 2, d).start()

    user_sum[...] = jnp.zeros_like(user_sum)
    for d in range(1, n_ia):
        spread_users(later_users, 2, d).wait_recv()
    for r in range(u_tiles):
        later_users_t[:, r * TILE : (r + 1) * TILE] = jnp.transpose(
            later_users[r * TILE : (r + 1) * TILE, :]
        )
    for d in range(1, n_au):
        spread_items(later_items, 2, d).wait_recv()

    def second_chunk(j, carry):
        k = lax.rem(a // chunk_peers + 1 + j, chunks)
        item_sum[...] = jnp.zeros_like(item_sum)

        def tile(t, inner):
            r = t // chunk_tiles
            c = t % chunk_tiles
            at_user = rows(r, TILE)
            at_item = rows(k * chunk_tiles + c, TILE)
            at_sum = rows(c, TILE)
            own_item = items[at_item, :]
            later_item = later_items[at_item, :]
            slope = nt_dot(users[at_user, :], later_item) + nt_dot(later_users[at_user, :], own_item)
            descent = (slope * weight[at_user, at_item]).astype(BF16)
            adj = adjacency[at_user, at_item]
            user_sum[at_user, :] += nn_dot(adj, later_item)
            user_sum[at_user, :EMB] += nn_dot(descent, own_item[:, EMB:])
            item_sum[:, at_sum] += nn_dot(later_users_t[:, at_user], adj)
            item_sum[EMB:, at_sum] += nn_dot(users_t[:EMB, at_user], descent)
            return inner

        lax.fori_loop(0, u_tiles * chunk_tiles, tile, 0)
        send_chunk(1, k)
        return carry

    lax.fori_loop(0, chunks, second_chunk, 0)

    user_stage[1] = user_sum[...].astype(BF16)
    for d in range(1, n_ia):
        user_part(1, d).start()

    total = item_total(1)
    layer = later_items[my_items, EMB:].astype(F32)
    item_final[...] = ((item_emb[...].astype(F32) + layer + total[:, :EMB]) / 3.0).astype(BF16)
    item_grad[...] = (item_cot[...].astype(F32) + total[:, EMB:]) / 3.0
    total = user_total(1)
    layer = later_users[my_users, :EMB].astype(F32)
    user_final[...] = ((user_emb[...].astype(F32) + layer + total[:, EMB:]) / 3.0).astype(BF16)
    user_grad[...] = (user_cot[...].astype(F32) + total[:, :EMB]) / 3.0

    for d in range(1, n_ia):
        spread_users(users, 0, d).wait_send()
        user_part(0, d).wait_send()
        spread_users(later_users, 2, d).wait_send()
        user_part(1, d).wait_send()
    for d in range(1, n_au):
        spread_items(items, 0, d).wait_send()
        item_part(0, d).wait_send()
        spread_items(later_items, 2, d).wait_send()
        item_part(1, d).wait_send()


def per_device(
    n_au,
    n_ia,
    user_emb,
    item_emb,
    user_cot,
    item_cot,
    user_degree,
    item_degree,
    tile_rows,
    tile_cols,
    tile_key,
    tile_count,
):
    us, it = user_emb.shape[0], item_emb.shape[0]
    u_block, i_block = us * n_ia, it * n_au
    u_tiles, i_tiles = u_block // TILE, i_block // TILE
    place = tile_rows.reshape(1, -1) * i_tiles + tile_cols.reshape(1, -1)
    slots = lax.broadcasted_iota(jnp.int32, place.shape, 1)
    place = jnp.where(slots < tile_count.reshape(1, 1), place, -1)
    found = place == lax.broadcasted_iota(jnp.int32, (u_tiles * i_tiles, 1), 0)
    keys = jnp.max(jnp.where(found, tile_key.reshape(1, -1), -1), axis=1)
    chunk = max(TILE, it)
    vmem = pl.BlockSpec(memory_space=pltpu.VMEM)
    smem = pl.BlockSpec(memory_space=pltpu.SMEM)
    return pl.pallas_call(
        functools.partial(kernel, n_au, n_ia),
        out_shape=(
            jax.ShapeDtypeStruct((us, EMB), BF16),
            jax.ShapeDtypeStruct((it, EMB), BF16),
            jax.ShapeDtypeStruct((us, EMB), F32),
            jax.ShapeDtypeStruct((it, EMB), F32),
        ),
        in_specs=[smem] + [vmem] * 6,
        out_specs=(vmem,) * 4,
        scratch_shapes=[
            pltpu.VMEM((u_block, 2 * EMB), BF16),
            pltpu.VMEM((i_block, 2 * EMB), BF16),
            pltpu.VMEM((u_block, 2 * EMB), BF16),
            pltpu.VMEM((i_block, 2 * EMB), BF16),
            pltpu.VMEM((2 * EMB, u_block), BF16),
            pltpu.VMEM((2 * EMB, u_block), BF16),
            pltpu.VMEM((u_block, i_block), F32),
            pltpu.VMEM((u_block, i_block), BF16),
            pltpu.VMEM((u_block, 128), F32),
            pltpu.VMEM((1, i_block), F32),
            pltpu.VMEM((u_block, 2 * EMB), F32),
            pltpu.VMEM((2 * EMB, chunk), F32),
            pltpu.VMEM((2, u_block, 2 * EMB), BF16),
            pltpu.VMEM((2, i_block, 2 * EMB), BF16),
            pltpu.VMEM((2, n_ia, us, 2 * EMB), BF16),
            pltpu.VMEM((2, n_au, it, 2 * EMB), BF16),
            pltpu.SemaphoreType.DMA((4, n_ia)),
            pltpu.SemaphoreType.DMA((4, n_ia)),
            pltpu.SemaphoreType.DMA((4, n_au)),
            pltpu.SemaphoreType.DMA((4, n_au)),
        ],
        compiler_params=pltpu.CompilerParams(
            collective_id=0, has_side_effects=True, vmem_limit_bytes=48 * 1024 * 1024
        ),
    )(
        keys,
        user_emb,
        item_emb,
        user_cot,
        item_cot,
        user_degree.reshape(1, -1),
        item_degree,
    )


def solution(mesh):
    shards = P(("au", "ia"), None)
    in_specs = (
        shards,
        shards,
        shards,
        shards,
        P("au"),
        P(None, "ia", None),
        P("au", "ia", None),
        P("au", "ia", None),
        P("au", "ia", None),
        P("au", "ia"),
    )
    return jax.shard_map(
        functools.partial(per_device, mesh.shape["au"], mesh.shape["ia"]),
        mesh=mesh,
        in_specs=in_specs,
        out_specs=(shards,) * 4,
        check_vma=False,
    )
```

time: 868 us -> 96.1 us (0.11); the launches traced: 853 us -> 95.7 us
  matrix products: 339 us -> 0 us
  waiting for transfers between devices: 185 us -> 0 us
  local copies, waits for them, and re-layouts: 138 us -> 6.61 us
  loops' own time: 122 us -> 0 us
  Pallas kernels: 0 us -> 86.3 us
  blocking collectives: 36.8 us -> 0 us
  other arithmetic: 18.2 us -> 1.42 us
  between operations: 14.3 us -> 1.33 us
    dot_general x264 -> x0, matrix products: 339 us -> none  [the longest x88 105 us: right_product(): lax.dot_general(matrix, other, (((1,), (1,)), ((), ())), preferred_elemen...]
    reduce_scatter x4 -> x0, waiting for transfers between devices: 162 us -> none  [the longest x2 84.5 us: sum_users(): lax.psum_scatter(partial_sum.astype(jnp.bfloat16), 'ia', scatter_dimensio...]
    another operation x2 -> x0, loops' own time: 122 us -> none  [the longest x1 62.5 us: per_device(): lax.fori_loop(0, occupied, second_joint, (user_zeros, item_zeros))]
    dynamic_slice x308 -> x0, local copies, waits for them, and re-layouts: 112 us -> none  [the longest x88 51.7 us: tile_starts(): return (row_ids[slot_index] * TILE, col_ids[slot_index] * TILE)]
    pallas_call x0 -> x1, Pallas kernels: none -> 86.3 us  [per_device(): pl.pallas_call(functools.partial(kernel, n_au, n_ia), out_shape=(jax.Shap...]
    all_gather x2 -> x0, blocking collectives: 36.8 us -> none  [gather_users(): return lax.all_gather(shard, 'ia', axis=0, tiled=True)]
    all_gather x2 -> x0, waiting for transfers between devices: 22.5 us -> none  [gather_items(): return lax.all_gather(shard, 'au', axis=0, tiled=True)]
    dynamic_update_slice x66 -> x0, local copies, waits for them, and re-layouts: 22.2 us -> none  [add_block(): return lax.dynamic_update_slice_in_dim(running, current + addend, offset, 0)]
  transfers between devices with their start and end apart: 6 -> 0, of which waited for: 6 -> 0; matrix products, arithmetic and copies ran while one was open for 1% -> 0% of each run, Pallas kernels for 0% -> 0%
where the time goes in v1:
time: 96.1 us; the launch traced here: 95.7 us
  Pallas kernels  86.3 us (90%)
  local copies, waits for them, and re-layouts  6.61 us (7%)
  other arithmetic  1.42 us (1%)
  between operations  1.33 us (1%)
    pallas_call x1, Pallas kernels, per_device(): pl.pallas_call(functools.partial(kernel, n_au, n_ia), out_shape=(jax.Shap...  86.3 us
    unnamed x16, local copies, waits for them, and re-layouts  6.61 us

profile of v1, /device:TPU:9, one launch (start us, length us, event | category | flops | bytes accessed | tf_op | source)
XLA Modules:
  0.0 95.7 jit_solution(9974653782488298066)
XLA Ops:
  0.6 0.0 copy-start.4
  1.3 0.7 compare_select_fusion
  2.0 0.7 select_reduce_fusion.keys
  2.7 0.0 copy-done.4
  2.7 0.0 copy-start
  2.7 0.9 copy-done
  3.6 0.0 copy-start.1
  3.6 0.9 copy-done.1
  4.5 0.0 copy-start.2
  4.5 0.8 copy-done.2
  5.3 0.0 copy-start.3
  5.3 0.8 copy-done.3
  6.1 0.0 copy-start.5
  6.1 0.7 copy-done.5
  6.7 86.3 %shard_map.129 = (bf16[128,128]{1,0:T(8,128)(2,1)S(1)}, bf16[512,128]{1,0:T(8,128)(2,1)S(1)}, f32[128,128]{1,0:T(8,128)S(1)}, f32[512,128]{1,0:T(8,128)S(1)}) custom-call(s32[32]{0:T(128)S(1)} %select_reduce_fusion.keys, bf16[128,128]{1,0:T(8,128)(2,1)S(1)} %copy-done.2, bf16[512,128]{1,0:T(8,128)(2,1)S(1)} %copy-done, bf16[128,128]{1,0:T(8,128)(2,1)S(1)} %copy-done.3, ...), custom_call_target="tpu_custom_call" | custom-call | tf_op jit(solution)/shard_map/pallas_call | solution.py:338
  93.1 0.6 copy.19
  93.7 0.7 copy.20
  94.4 0.6 copy.21
  95.0 0.7 copy.22
Async XLA Ops:
  0.6 2.1 %copy-start.4 = (s32[4,1,512]{2,1,0:T(1,128)S(1)}, s32[4,1,512]{2,1,0:T(1,128)}, u32[]{:S(2)}) copy-start(s32[4,1,512]{2,1,0:T(1,128)} %item_degree.1) | copy-start | bytes 24580
  2.7 0.9 copy-start
  3.6 0.9 copy-start.1
  4.5 0.8 copy-start.2
  5.3 0.8 copy-start.3
  6.1 0.7 copy-start.5

commit v2 on v1

--- a/solution.py
+++ b/solution.py
@@ -25,13 +25,16 @@
 def kernel(
     n_au,
     n_ia,
-    keys,
     user_emb,
     item_emb,
     user_cot,
     item_cot,
-    user_degree,
-    item_degree,
+    user_degree_hbm,
+    item_degree_hbm,
+    tile_rows_hbm,
+    tile_cols_hbm,
+    tile_key_hbm,
+    tile_count_hbm,
     user_final,
     item_final,
     user_grad,
@@ -50,8 +53,17 @@
     item_sum,
     user_stage,
     item_stage,
+    user_pair,
+    user_send,
     user_recv,
     item_recv,
+    user_degree,
+    item_degree,
+    tile_rows,
+    tile_cols,
+    tile_key,
+    tile_count,
+    local_sem,
     user_send_sem,
     user_recv_sem,
     item_send_sem,
@@ -76,27 +88,70 @@
     my_users = rows(i, us)
     my_items = rows(a, it)
 
-    users[my_users, :EMB] = user_emb[...]
-    users[my_users, EMB:] = user_cot[...]
-    items[my_items, :EMB] = item_cot[...]
-    items[my_items, EMB:] = item_emb[...]
+    local = [
+        pltpu.make_async_copy(src, dst, local_sem.at[n])
+        for n, (src, dst) in enumerate(
+            (
+                (user_emb, users.at[my_users, :EMB]),
+                (user_cot, users.at[my_users, EMB:]),
+                (item_cot, items.at[my_items, :EMB]),
+                (item_emb, items.at[my_items, EMB:]),
+                (user_degree_hbm, user_degree),
+                (item_degree_hbm, item_degree),
+                (tile_rows_hbm, tile_rows),
+                (tile_cols_hbm, tile_cols),
+                (tile_key_hbm, tile_key),
+                (tile_count_hbm, tile_count),
+            )
+        )
+    ]
+    for copy in local:
+        copy.start()
+
+    nz = n_ia // 2
+    sibling = i + 1 - 2 * lax.rem(i, 2)
 
     barrier = pltpu.get_barrier_semaphore()
-    for d in range(1, n_ia):
-        pl.semaphore_signal(barrier, inc=1, device_id=(a, lax.rem(i + d, n_ia)), device_id_type=MESH)
+    pl.semaphore_signal(barrier, inc=1, device_id=(a, sibling), device_id_type=MESH)
+    for e in range(1, nz):
+        pl.semaphore_signal(
+            barrier, inc=1, device_id=(a, lax.rem(i + 2 * e, n_ia)), device_id_type=MESH
+        )
     for d in range(1, n_au):
         pl.semaphore_signal(barrier, inc=1, device_id=(lax.rem(a + d, n_au), i), device_id_type=MESH)
-    pl.semaphore_wait(barrier, n_ia + n_au - 2)
-
-    def spread_users(ref, phase, d):
+    pl.semaphore_wait(barrier, nz + n_au - 1)
+
+    def user_copy(src, dst, phase, d, peer):
         return pltpu.make_async_remote_copy(
-            src_ref=ref.at[my_users],
-            dst_ref=ref.at[my_users],
+            src_ref=src,
+            dst_ref=dst,
             send_sem=user_send_sem.at[phase, d],
             recv_sem=user_recv_sem.at[phase, d],
-            device_id=(a, lax.rem(i + d, n_ia)),
+            device_id=(a, peer),
             device_id_type=MESH,
         )
+
+    def spread_along(ref, phase, e):
+        part = ref.at[my_users]
+        return user_copy(part, part, phase, 2 * e, lax.rem(i + 2 * e, n_ia))
+
+    def spread_across(ref, phase, e):
+        part = ref.at[rows(lax.rem(i + n_ia - 2 * e, n_ia), us)]
+        return user_copy(part, part, phase, 2 * e + 1, sibling)
+
+    def spread_start(ref, phase):
+        for e in range(1, nz):
+            spread_along(ref, phase, e).start()
+        spread_across(ref, phase, 0).start()
+
+    def spread_forward(ref, phase):
+        for e in range(1, nz):
+            spread_along(ref, phase, e).wait_recv()
+            spread_across(ref, phase, e).start()
+
+    def spread_end(ref, phase):
+        for e in range(nz):
+            spread_across(ref, phase, e).wait_recv()
 
     def spread_items(ref, phase, d):
         return pltpu.make_async_remote_copy(
@@ -108,16 +163,36 @@
             device_id_type=MESH,
         )
 
-    def user_part(layer, d):
-        peer = lax.rem(i + d, n_ia)
-        return pltpu.make_async_remote_copy(
-            src_ref=user_stage.at[layer, rows(peer, us)],
-            dst_ref=user_recv.at[layer, d],
-            send_sem=user_send_sem.at[2 * layer + 1, d],
-            recv_sem=user_recv_sem.at[2 * layer + 1, d],
-            device_id=(a, peer),
-            device_id_type=MESH,
-        )
+    def pair_part(layer, e):
+        owner = lax.rem(sibling + 2 * e, n_ia)
+        return user_copy(
+            user_stage.at[layer, rows(owner, us)],
+            user_pair.at[layer, e],
+            2 * layer + 1,
+            2 * e + 1,
+            sibling,
+        )
+
+    def user_part(layer, e):
+        return user_copy(
+            user_send.at[layer, e],
+            user_recv.at[layer, e],
+            2 * layer + 1,
+            2 * e,
+            lax.rem(i + 2 * e, n_ia),
+        )
+
+    def send_users(layer):
+        user_stage[layer] = user_sum[...].astype(BF16)
+        order = list(range(1, nz)) + [0]
+        for e in order:
+            pair_part(layer, e).start()
+        for e in order:
+            pair_part(layer, e).wait_recv()
+            if e:
+                own = user_stage[layer, rows(lax.rem(i + 2 * e, n_ia), us), :].astype(F32)
+                user_send[layer, e] = (own + user_pair[layer, e].astype(F32)).astype(BF16)
+                user_part(layer, e).start()
 
     def item_part(layer, d):
         peer = lax.rem(a + d, n_au)
@@ -130,10 +205,15 @@
             device_id_type=MESH,
         )
 
-    for d in range(1, n_ia):
-        spread_users(users, 0, d).start()
+    for copy in local:
+        copy.wait()
+    spread_start(users, 0)
     for d in range(1, n_au):
         spread_items(items, 0, d).start()
+
+    slots = lax.broadcasted_iota(jnp.int32, tile_key.shape, 1)
+    places = jnp.where(slots < tile_count[...], tile_rows[...] * i_tiles + tile_cols[...], -1)
+    slot_keys = tile_key[...]
 
     scale_row = lax.rsqrt(user_degree[...].astype(F32))
     for r in range(u_tiles):
@@ -154,7 +234,7 @@
     def mask_tile(t, carry):
         r = t // i_tiles
         c = t % i_tiles
-        key = keys[t]
+        key = jnp.max(jnp.where(places == t, slot_keys, -1), axis=1, keepdims=True)
         target = jnp.where(key >= 0, 0, 8)
         h1 = fold(row_ids + key * 263)
         h1 = jnp.where(h1 >= 8191, h1 - 8191, h1)
@@ -172,11 +252,13 @@
             )
         return carry
 
-    lax.fori_loop(0, u_tiles * i_tiles, mask_tile, 0)
+    tiles = u_tiles * i_tiles
+    lax.fori_loop(0, tiles // 2, mask_tile, 0)
+    spread_forward(users, 0)
+    lax.fori_loop(tiles // 2, tiles, mask_tile, 0)
 
     user_sum[...] = jnp.zeros_like(user_sum)
-    for d in range(1, n_ia):
-        spread_users(users, 0, d).wait_recv()
+    spread_end(users, 0)
     for r in range(u_tiles):
         users_t[:, r * TILE : (r + 1) * TILE] = jnp.transpose(users[r * TILE : (r + 1) * TILE, :])
     for d in range(1, n_au):
@@ -212,21 +294,19 @@
             item_sum[:, rows(c, TILE)] += nn_dot(users_t[:, at_user], adj)
             return inner
 
-        lax.fori_loop(0, u_tiles * chunk_tiles, tile, 0)
+        lax.fori_loop(0, u_tiles * chunk_tiles, tile, 0, unroll=4)
         send_chunk(0, k)
         return carry
 
     lax.fori_loop(0, chunks, first_chunk, 0)
 
-    user_stage[0] = user_sum[...].astype(BF16)
-    for d in range(1, n_ia):
-        user_part(0, d).start()
+    send_users(0)
 
     def user_total(layer):
-        total = user_stage[layer, my_users, :].astype(F32)
-        for d in range(1, n_ia):
-            user_part(layer, d).wait_recv()
-            total = total + user_recv[layer, d].astype(F32)
+        total = user_stage[layer, my_users, :].astype(F32) + user_pair[layer, 0].astype(F32)
+        for e in range(1, nz):
+            user_part(layer, e).wait_recv()
+            total = total + user_recv[layer, e].astype(F32)
         return total
 
     def item_total(layer):
@@ -238,19 +318,18 @@
         return total
 
     total = item_total(0)
-    later_items[my_items, :EMB] = (item_cot[...].astype(F32) + total[:, EMB:]).astype(BF16)
+    later_items[my_items, :EMB] = (items[my_items, :EMB].astype(F32) + total[:, EMB:]).astype(BF16)
     later_items[my_items, EMB:] = total[:, :EMB].astype(BF16)
     for d in range(1, n_au):
         spread_items(later_items, 2, d).start()
     total = user_total(0)
     later_users[my_users, :EMB] = total[:, EMB:].astype(BF16)
-    later_users[my_users, EMB:] = (user_cot[...].astype(F32) + total[:, :EMB]).astype(BF16)
-    for d in range(1, n_ia):
-        spread_users(later_users, 2, d).start()
+    later_users[my_users, EMB:] = (users[my_users, EMB:].astype(F32) + total[:, :EMB]).astype(BF16)
+    spread_start(later_users, 2)
 
     user_sum[...] = jnp.zeros_like(user_sum)
-    for d in range(1, n_ia):
-        spread_users(later_users, 2, d).wait_recv()
+    spread_forward(later_users, 2)
+    spread_end(later_users, 2)
     for r in range(u_tiles):
         later_users_t[:, r * TILE : (r + 1) * TILE] = jnp.transpose(
             later_users[r * TILE : (r + 1) * TILE, :]
@@ -279,30 +358,33 @@
             item_sum[EMB:, at_sum] += nn_dot(users_t[:EMB, at_user], descent)
             return inner
 
-        lax.fori_loop(0, u_tiles * chunk_tiles, tile, 0)
+        lax.fori_loop(0, u_tiles * chunk_tiles, tile, 0, unroll=4)
         send_chunk(1, k)
         return carry
 
     lax.fori_loop(0, chunks, second_chunk, 0)
 
-    user_stage[1] = user_sum[...].astype(BF16)
-    for d in range(1, n_ia):
-        user_part(1, d).start()
+    send_users(1)
 
     total = item_total(1)
     layer = later_items[my_items, EMB:].astype(F32)
-    item_final[...] = ((item_emb[...].astype(F32) + layer + total[:, :EMB]) / 3.0).astype(BF16)
-    item_grad[...] = (item_cot[...].astype(F32) + total[:, EMB:]) / 3.0
+    item_final[...] = ((items[my_items, EMB:].astype(F32) + layer + total[:, :EMB]) / 3.0).astype(BF16)
+    item_grad[...] = (items[my_items, :EMB].astype(F32) + total[:, EMB:]) / 3.0
     total = user_total(1)
     layer = later_users[my_users, :EMB].astype(F32)
-    user_final[...] = ((user_emb[...].astype(F32) + layer + total[:, EMB:]) / 3.0).astype(BF16)
-    user_grad[...] = (user_cot[...].astype(F32) + total[:, :EMB]) / 3.0
-
-    for d in range(1, n_ia):
-        spread_users(users, 0, d).wait_send()
-        user_part(0, d).wait_send()
-        spread_users(later_users, 2, d).wait_send()
-        user_part(1, d).wait_send()
+    user_final[...] = ((users[my_users, :EMB].astype(F32) + layer + total[:, EMB:]) / 3.0).astype(BF16)
+    user_grad[...] = (users[my_users, EMB:].astype(F32) + total[:, :EMB]) / 3.0
+
+    for e in range(nz):
+        spread_across(users, 0, e).wait_send()
+        spread_across(later_users, 2, e).wait_send()
+        pair_part(0, e).wait_send()
+        pair_part(1, e).wait_send()
+    for e in range(1, nz):
+        spread_along(users, 0, e).wait_send()
+        spread_along(later_users, 2, e).wait_send()
+        user_part(0, e).wait_send()
+        user_part(1, e).wait_send()
     for d in range(1, n_au):
         spread_items(items, 0, d).wait_send()
         item_part(0, d).wait_send()
@@ -326,15 +408,9 @@
 ):
     us, it = user_emb.shape[0], item_emb.shape[0]
     u_block, i_block = us * n_ia, it * n_au
-    u_tiles, i_tiles = u_block // TILE, i_block // TILE
-    place = tile_rows.reshape(1, -1) * i_tiles + tile_cols.reshape(1, -1)
-    slots = lax.broadcasted_iota(jnp.int32, place.shape, 1)
-    place = jnp.where(slots < tile_count.reshape(1, 1), place, -1)
-    found = place == lax.broadcasted_iota(jnp.int32, (u_tiles * i_tiles, 1), 0)
-    keys = jnp.max(jnp.where(found, tile_key.reshape(1, -1), -1), axis=1)
     chunk = max(TILE, it)
     vmem = pl.BlockSpec(memory_space=pltpu.VMEM)
-    smem = pl.BlockSpec(memory_space=pltpu.SMEM)
+    slots = tile_key.shape[-1]
     return pl.pallas_call(
         functools.partial(kernel, n_au, n_ia),
         out_shape=(
@@ -343,7 +419,7 @@
             jax.ShapeDtypeStruct((us, EMB), F32),
             jax.ShapeDtypeStruct((it, EMB), F32),
         ),
-        in_specs=[smem] + [vmem] * 6,
+        in_specs=[pl.BlockSpec(memory_space=pl.ANY)] * 10,
         out_specs=(vmem,) * 4,
         scratch_shapes=[
             pltpu.VMEM((u_block, 2 * EMB), BF16),
@@ -360,8 +436,17 @@
             pltpu.VMEM((2 * EMB, chunk), F32),
             pltpu.VMEM((2, u_block, 2 * EMB), BF16),
             pltpu.VMEM((2, i_block, 2 * EMB), BF16),
-            pltpu.VMEM((2, n_ia, us, 2 * EMB), BF16),
+            pltpu.VMEM((2, n_ia // 2, us, 2 * EMB), BF16),
+            pltpu.VMEM((2, n_ia // 2, us, 2 * EMB), BF16),
+            pltpu.VMEM((2, n_ia // 2, us, 2 * EMB), BF16),
             pltpu.VMEM((2, n_au, it, 2 * EMB), BF16),
+            pltpu.VMEM((1, u_block), jnp.int32),
+            pltpu.VMEM((n_au, 1, it), jnp.int32),
+            pltpu.VMEM((1, slots), jnp.int32),
+            pltpu.VMEM((1, slots), jnp.int32),
+            pltpu.VMEM((1, slots), jnp.int32),
+            pltpu.VMEM((1, 1), jnp.int32),
+            pltpu.SemaphoreType.DMA((10,)),
             pltpu.SemaphoreType.DMA((4, n_ia)),
             pltpu.SemaphoreType.DMA((4, n_ia)),
             pltpu.SemaphoreType.DMA((4, n_au)),
@@ -371,13 +456,16 @@
             collective_id=0, has_side_effects=True, vmem_limit_bytes=48 * 1024 * 1024
         ),
     )(
-        keys,
         user_emb,
         item_emb,
         user_cot,
         item_cot,
         user_degree.reshape(1, -1),
         item_degree,
+        tile_rows.reshape(1, -1),
+        tile_cols.reshape(1, -1),
+        tile_key.reshape(1, -1),
+        tile_count,
     )
 
 

time: 96.1 us -> 74.5 us (0.78)
  Pallas kernels: 86.3 us -> 64.3 us
  other arithmetic: 1.42 us -> 0 us
  local copies, waits for them, and re-layouts: 6.61 us -> 7.92 us
    pallas_call x1, Pallas kernels: 86.3 us -> 64.3 us  [per_device(): pl.pallas_call(functools.partial(kernel, n_au, n_ia), out_shape=(jax.Shap...]
    unnamed x16 -> x22, local copies, waits for them, and re-layouts: 6.61 us -> 7.92 us
where the time goes in v2:
time: 74.5 us; the launch traced here: 73.5 us
  Pallas kernels  64.3 us (86%)
  local copies, waits for them, and re-layouts  7.92 us (11%)
  between operations  1.33 us (2%)
    pallas_call x1, Pallas kernels, per_device(): pl.pallas_call(functools.partial(kernel, n_au, n_ia), out_shape=(jax.Shap...  64.3 us
    unnamed x22, local copies, waits for them, and re-layouts  7.92 us

profile of v2, /device:TPU:9, one launch (start us, length us, event | category | flops | bytes accessed | tf_op | source)
XLA Modules:
  0.0 73.5 jit_solution(17352936310485878847)
XLA Ops:
  0.6 0.0 copy-start.4
  1.3 0.0 copy-start.6
  1.3 0.0 copy-start.7
  1.3 0.0 copy-done.4
  1.3 0.6 copy-done.6
  2.0 0.0 copy-done.7
  2.0 0.0 copy-start
  2.0 0.9 %copy-done = bf16[512,128]{1,0:T(8,128)(2,1)S(1)} copy-done((bf16[512,128]{1,0:T(8,128)(2,1)S(1)}, bf16[512,128]{1,0:T(8,128)(2,1)}, u32[]{:S(2)}) %copy-start) | copy-done | bytes 131096
  2.9 0.0 copy-start.1
  2.9 0.9 %copy-done.1 = bf16[512,128]{1,0:T(8,128)(2,1)S(1)} copy-done((bf16[512,128]{1,0:T(8,128)(2,1)S(1)}, bf16[512,128]{1,0:T(8,128)(2,1)}, u32[]{:S(2)}) %copy-start.1) | copy-done | bytes 131096
  3.8 0.0 copy-start.2
  3.8 0.8 %copy-done.2 = bf16[128,128]{1,0:T(8,128)(2,1)S(1)} copy-done((bf16[128,128]{1,0:T(8,128)(2,1)S(1)}, bf16[128,128]{1,0:T(8,128)(2,1)}, u32[]{:S(2)}) %copy-start.2) | copy-done | bytes 32792
  4.5 0.0 copy-start.3
  4.5 0.8 %copy-done.3 = bf16[128,128]{1,0:T(8,128)(2,1)S(1)} copy-done((bf16[128,128]{1,0:T(8,128)(2,1)S(1)}, bf16[128,128]{1,0:T(8,128)(2,1)}, u32[]{:S(2)}) %copy-start.3) | copy-done | bytes 32792
  5.3 0.0 copy-start.5
  5.3 0.7 copy-done.5
  6.0 0.0 copy-start.8
  6.0 0.7 copy-done.8
  6.6 64.3 %shard_map.129 = (bf16[128,128]{1,0:T(8,128)(2,1)S(1)}, bf16[512,128]{1,0:T(8,128)(2,1)S(1)}, f32[128,128]{1,0:T(8,128)S(1)}, f32[512,128]{1,0:T(8,128)S(1)}) custom-call(bf16[128,128]{1,0:T(8,128)(2,1)S(1)} %copy-done.2, bf16[512,128]{1,0:T(8,128)(2,1)S(1)} %copy-done, bf16[128,128]{1,0:T(8,128)(2,1)S(1)} %copy-done.3, bf16[512,128]{1,0:T(8,128)(2,1)S(1)} %copy-done.1, ...), custom_call_target="tpu_custom_call" | custom-call | tf_op jit(solution)/shard_map/pallas_call | solution.py:414
  70.9 0.6 copy.19
  71.5 0.7 copy.20
  72.2 0.6 copy.21
  72.8 0.7 copy.22
Async XLA Ops:
  0.6 0.7 copy-start.4
  1.3 0.7 copy-start.6
  1.3 0.7 copy-start.7
  2.0 0.9 %copy-start = (bf16[512,128]{1,0:T(8,128)(2,1)S(1)}, bf16[512,128]{1,0:T(8,128)(2,1)}, u32[]{:S(2)}) copy-start(bf16[512,128]{1,0:T(8,128)(2,1)} %item_emb.1) | copy-start | bytes 393220
  2.9 0.9 %copy-start.1 = (bf16[512,128]{1,0:T(8,128)(2,1)S(1)}, bf16[512,128]{1,0:T(8,128)(2,1)}, u32[]{:S(2)}) copy-start(bf16[512,128]{1,0:T(8,128)(2,1)} %item_cot.1) | copy-start | bytes 393220
  3.8 0.8 %copy-start.2 = (bf16[128,128]{1,0:T(8,128)(2,1)S(1)}, bf16[128,128]{1,0:T(8,128)(2,1)}, u32[]{:S(2)}) copy-start(bf16[128,128]{1,0:T(8,128)(2,1)} %user_emb.1) | copy-start | bytes 98308
  4.5 0.8 %copy-start.3 = (bf16[128,128]{1,0:T(8,128)(2,1)S(1)}, bf16[128,128]{1,0:T(8,128)(2,1)}, u32[]{:S(2)}) copy-start(bf16[128,128]{1,0:T(8,128)(2,1)} %user_cot.1) | copy-start | bytes 98308
  5.3 0.7 copy-start.5
  6.0 0.7 copy-start.8

commit v3 on v2

--- a/solution.py
+++ b/solution.py
@@ -208,7 +208,7 @@
     for copy in local:
         copy.wait()
     spread_start(users, 0)
-    for d in range(1, n_au):
+    for d in reversed(range(1, n_au)):
         spread_items(items, 0, d).start()
 
     slots = lax.broadcasted_iota(jnp.int32, tile_key.shape, 1)
@@ -261,8 +261,14 @@
     spread_end(users, 0)
     for r in range(u_tiles):
         users_t[:, r * TILE : (r + 1) * TILE] = jnp.transpose(users[r * TILE : (r + 1) * TILE, :])
-    for d in range(1, n_au):
-        spread_items(items, 0, d).wait_recv()
+
+    def await_chunk(ref, phase, k):
+        for p in range(chunk_peers):
+            d = lax.rem(a - k * chunk_peers - p + n_au, n_au)
+
+            @pl.when(d != 0)
+            def _():
+                spread_items(ref, phase, d).wait_recv()
 
     def send_chunk(layer, k):
         for p in range(chunk_peers):
@@ -277,6 +283,7 @@
 
     def first_chunk(j, carry):
         k = lax.rem(a // chunk_peers + 1 + j, chunks)
+        await_chunk(items, 0, k)
         item_sum[...] = jnp.zeros_like(item_sum)
 
         def tile(t, inner):
@@ -320,7 +327,7 @@
     total = item_total(0)
     later_items[my_items, :EMB] = (items[my_items, :EMB].astype(F32) + total[:, EMB:]).astype(BF16)
     later_items[my_items, EMB:] = total[:, :EMB].astype(BF16)
-    for d in range(1, n_au):
+    for d in reversed(range(1, n_au)):
         spread_items(later_items, 2, d).start()
     total = user_total(0)
     later_users[my_users, :EMB] = total[:, EMB:].astype(BF16)
@@ -334,11 +341,10 @@
         later_users_t[:, r * TILE : (r + 1) * TILE] = jnp.transpose(
             later_users[r * TILE : (r + 1) * TILE, :]
         )
-    for d in range(1, n_au):
-        spread_items(later_items, 2, d).wait_recv()
 
     def second_chunk(j, carry):
         k = lax.rem(a // chunk_peers + 1 + j, chunks)
+        await_chunk(later_items, 2, k)
         item_sum[...] = jnp.zeros_like(item_sum)
 
         def tile(t, inner):

time: 74.5 us -> 74.2 us (level)
  no operation moved by 1% of the time
where the time goes in v3:
time: 74.2 us; the launch traced here: 72.9 us
  Pallas kernels  63.6 us (86%)
  local copies, waits for them, and re-layouts  7.92 us (11%)
  between operations  1.33 us (2%)
    pallas_call x1, Pallas kernels, per_device(): pl.pallas_call(functools.partial(kernel, n_au, n_ia), out_shape=(jax.Shap...  63.6 us
    unnamed x22, local copies, waits for them, and re-layouts  7.92 us

profile of v3, /device:TPU:9, one launch (start us, length us, event | category | flops | bytes accessed | tf_op | source)
XLA Modules:
  0.0 72.9 jit_solution(15889581927220602893)
XLA Ops:
  0.6 0.0 copy-start.4
  1.3 0.0 copy-start.6
  1.3 0.0 copy-start.7
  1.3 0.0 copy-done.4
  1.3 0.6 copy-done.6
  2.0 0.0 copy-done.7
  2.0 0.0 copy-start
  2.0 0.9 %copy-done = bf16[512,128]{1,0:T(8,128)(2,1)S(1)} copy-done((bf16[512,128]{1,0:T(8,128)(2,1)S(1)}, bf16[512,128]{1,0:T(8,128)(2,1)}, u32[]{:S(2)}) %copy-start) | copy-done | bytes 131096
  2.9 0.0 copy-start.1
  2.9 0.9 %copy-done.1 = bf16[512,128]{1,0:T(8,128)(2,1)S(1)} copy-done((bf16[512,128]{1,0:T(8,128)(2,1)S(1)}, bf16[512,128]{1,0:T(8,128)(2,1)}, u32[]{:S(2)}) %copy-start.1) | copy-done | bytes 131096
  3.8 0.0 copy-start.2
  3.8 0.8 %copy-done.2 = bf16[128,128]{1,0:T(8,128)(2,1)S(1)} copy-done((bf16[128,128]{1,0:T(8,128)(2,1)S(1)}, bf16[128,128]{1,0:T(8,128)(2,1)}, u32[]{:S(2)}) %copy-start.2) | copy-done | bytes 32792
  4.5 0.0 copy-start.3
  4.5 0.8 %copy-done.3 = bf16[128,128]{1,0:T(8,128)(2,1)S(1)} copy-done((bf16[128,128]{1,0:T(8,128)(2,1)S(1)}, bf16[128,128]{1,0:T(8,128)(2,1)}, u32[]{:S(2)}) %copy-start.3) | copy-done | bytes 32792
  5.3 0.0 copy-start.5
  5.3 0.7 copy-done.5
  6.0 0.0 copy-start.8
  6.0 0.7 copy-done.8
  6.6 63.6 %shard_map.129 = (bf16[128,128]{1,0:T(8,128)(2,1)S(1)}, bf16[512,128]{1,0:T(8,128)(2,1)S(1)}, f32[128,128]{1,0:T(8,128)S(1)}, f32[512,128]{1,0:T(8,128)S(1)}) custom-call(bf16[128,128]{1,0:T(8,128)(2,1)S(1)} %copy-done.2, bf16[512,128]{1,0:T(8,128)(2,1)S(1)} %copy-done, bf16[128,128]{1,0:T(8,128)(2,1)S(1)} %copy-done.3, bf16[512,128]{1,0:T(8,128)(2,1)S(1)} %copy-done.1, ...), custom_call_target="tpu_custom_call" | custom-call | tf_op jit(solution)/shard_map/pallas_call | solution.py:420
  70.2 0.6 copy.19
  70.9 0.7 copy.20
  71.5 0.6 copy.21
  72.2 0.7 copy.22
Async XLA Ops:
  0.6 0.7 copy-start.4
  1.3 0.7 copy-start.6
  1.3 0.7 copy-start.7
  2.0 0.9 %copy-start = (bf16[512,128]{1,0:T(8,128)(2,1)S(1)}, bf16[512,128]{1,0:T(8,128)(2,1)}, u32[]{:S(2)}) copy-start(bf16[512,128]{1,0:T(8,128)(2,1)} %item_emb.1) | copy-start | bytes 393220
  2.9 0.9 %copy-start.1 = (bf16[512,128]{1,0:T(8,128)(2,1)S(1)}, bf16[512,128]{1,0:T(8,128)(2,1)}, u32[]{:S(2)}) copy-start(bf16[512,128]{1,0:T(8,128)(2,1)} %item_cot.1) | copy-start | bytes 393220
  3.8 0.8 %copy-start.2 = (bf16[128,128]{1,0:T(8,128)(2,1)S(1)}, bf16[128,128]{1,0:T(8,128)(2,1)}, u32[]{:S(2)}) copy-start(bf16[128,128]{1,0:T(8,128)(2,1)} %user_emb.1) | copy-start | bytes 98308
  4.5 0.8 %copy-start.3 = (bf16[128,128]{1,0:T(8,128)(2,1)S(1)}, bf16[128,128]{1,0:T(8,128)(2,1)}, u32[]{:S(2)}) copy-start(bf16[128,128]{1,0:T(8,128)(2,1)} %user_cot.1) | copy-start | bytes 98308
  5.3 0.7 copy-start.5
  6.0 0.7 copy-start.8
